TPU v7x, 32 devices: a whole 2x2x4 slice. The times are simulated.
32 devices in a mesh: dp: 4 (over y, x), pipe: 4 (over z), tensor: 2 (over core).
Axes of the slice: x: 2, y: 2, z: 4, core: 2. Of those that a mesh axis runs over, the one named last changes fastest.
Arguments:
- hidden: bfloat16 [4, 256, 14336], P('pipe', 'dp', 'tensor'), parts along dimension 1, may hold values from -6 to 6
- residual: bfloat16 [4, 256, 4096], P('pipe', ('dp', 'tensor')), parts along dimension 1, may hold values from -6 to 6
- norm_gain: float32 [4, 4096], P('pipe'), may hold values from 0.5 to 1.5
- down_weight: bfloat16 [4, 14336, 4096], P('pipe', 'tensor'), may hold values from -0.046875 to 0.046875
- qkv_weight: bfloat16 [4, 4096, 6144], P('pipe', None, 'tensor'), may hold values from -0.09375 to 0.09375
Outputs:
- section_output: bfloat16 [4, 256, 4096], P('pipe', ('dp', 'tensor')), parts along dimension 1
- projections: bfloat16 [4, 256, 6144], P('pipe', 'dp', 'tensor'), parts along dimension 1
There are 4 independent parts, one for each index of `dp`. A program takes and returns all parts, laid end to end along the dimension named above; an argument that names none is the same for every part. Nothing has to cross between parts.
All inputs are finite; a program needn't handle non-finite values.
Results may differ from a plain program's by a relative error of at most 0.022.
Values may be sent and summed in bfloat16 or wider, within the bound.
A program may use at most 128 MiB of HBM per device.

v0:
```python
import jax
import jax.numpy as jnp
from jax import lax
from jax.sharding import PartitionSpec as P


def passed_along(value, axis, steps):
    count = lax.axis_size(axis)
    pairs = [(source, (source + steps) % count) for source in range(count)]
    return lax.ppermute(value, axis, pairs)


def normalize(values, gain_row):
    wide = values.astype(jnp.float32)
    scaler = lax.rsqrt(jnp.mean(wide * wide, axis=-1, keepdims=True) + 1e-05)
    return (wide * scaler * gain_row).astype(jnp.bfloat16)


def shards(hidden, residual, norm_gain, down_weight, qkv_weight):
    hidden_rows = hidden[0]
    resid_rows = residual[0]
    gain_row = norm_gain[0]
    down_local = down_weight[0]
    qkv_local = qkv_weight[0]
    tok_rows = resid_rows.shape[0]
    resid_full = lax.all_gather(resid_rows, "tensor", axis=0, tiled=True)
    summed = lax.psum(
        jnp.dot(hidden_rows, down_local, preferred_element_type=jnp.float32).astype(jnp.bfloat16),
        "tensor",
    ).astype(jnp.float32)
    full_rows = (resid_full.astype(jnp.float32) + summed).astype(jnp.bfloat16)
    offset = lax.axis_index("tensor") * tok_rows
    section_output = lax.dynamic_slice_in_dim(full_rows, offset, tok_rows, 0)
    arrived = passed_along(full_rows, "pipe", 1)
    normed = normalize(arrived, gain_row)
    projections = jnp.dot(normed, qkv_local, preferred_element_type=jnp.float32).astype(
        jnp.bfloat16
    )
    return (section_output[None], projections[None])


def solution(mesh):
    return jax.shard_map(
        shards,
        mesh=mesh,
        in_specs=(
            P("pipe", "dp", "tensor"),
            P("pipe", ("dp", "tensor"), None),
            P("pipe", None),
            P("pipe", "tensor", None),
            P("pipe", None, "tensor"),
        ),
        out_specs=(P("pipe", ("dp", "tensor"), None), P("pipe", "dp", "tensor")),
        check_vma=False,
    )
```

profile of v0, /device:TPU:0, one launch (start us, length us, event | category | flops | bytes accessed | tf_op | source)
XLA Modules:
  0.0 87.9 jit_solution(12582749221237585882)
XLA Ops:
  7.2 0.0 copy-start
  7.2 0.0 copy-start.1
  7.2 0.0 copy-start.2
  7.2 0.0 all-reduce.2.cloned.1.call-start
  7.2 1.1 %copy-done = bf16[1,64,7168]{2,1,0:T(8,128)(2,1)S(1)} copy-done((bf16[1,64,7168]{2,1,0:T(8,128)(2,1)S(1)}, bf16[1,64,7168]{2,1,0:T(8,128)(2,1)}, u32[]{:S(2)}) %copy-start) | copy-done | bytes 917528
  8.3 22.4 %fusion.4 = bf16[64,4096]{1,0:T(8,128)(2,1)} fusion(bf16[1,7168,4096]{2,1,0:T(8,128)(2,1)} %param.8, bf16[1,64,7168]{2,1,0:T(8,128)(2,1)S(1)} %copy-done), kind=kOutput, calls=%fused_computation.4 | convolution fusion | flops 3758358528 | bytes 60162048 | tf_op jit(solution)/shard_map/dot_general | solution.py:28
  30.7 0.0 all-reduce.2.cloned.1.call-update
  30.8 0.0 copy-done.1
  30.8 2.3 %all-gather = bf16[1,64,4096]{2,1,0:T(8,128)(2,1)S(1)} all-gather(bf16[1,32,4096]{2,1,0:T(8,128)(2,1)S(1)} %copy-done.1), channel_id=2, replica_groups=mesh['dp'=4,'pipe'=4,'tensor'=2] {'tensor'}, dimensions={1}, use_global_device_ids=true | all-gather | bytes 786432 | tf_op jit(solution)/shard_map/all_gather | solution.py:26
  33.0 19.3 %all-reduce.2.cloned.1.call-done = bf16[64,4096]{1,0:T(8,128)(2,1)} async-done(((bf16[64,4096]{1,0:T(8,128)(2,1)}), bf16[64,4096]{1,0:T(8,128)(2,1)}) %all-reduce.2.cloned.1.call-update) | async-done | bytes 524304 | tf_op jit(solution)/shard_map/psum | solution.py:27
  52.3 1.2 %fusion.16 = bf16[64,4096]{1,0:T(8,128)(2,1)S(1)} fusion(bf16[64,4096]{1,0:T(8,128)(2,1)} %all-reduce.2.cloned.1.call-done, bf16[1,64,4096]{2,1,0:T(8,128)(2,1)S(1)} %all-gather), kind=kLoop, calls=%fused_computation.13 | loop fusion | flops 1048576 | bytes 1572864 | tf_op jit(solution)/shard_map/convert_element_type | solution.py:31
  53.5 1.8 %collective-permute-start = (bf16[64,4096]{1,0:T(8,128)(2,1)S(1)}, bf16[64,4096]{1,0:T(8,128)(2,1)S(1)}, u32[]{:S(2)}, u32[]{:S(2)}) collective-permute-start(bf16[64,4096]{1,0:T(8,128)(2,1)S(1)} %fusion.16), channel_id=1, source_target_pairs={{0,2},{2,4},{4,6},{6,0},{1,3},{3,5},{5,7},{7,1},{8,10},{10,12},{12... | collective-permute-start | bytes 1572872 | tf_op jit(solution)/shard_map/ppermute | solution.py:10
  55.3 0.7 dynamic-slice_bitcast_fusion
  56.0 13.5 %collective-permute-done = bf16[64,4096]{1,0:T(8,128)(2,1)S(1)} collective-permute-done((bf16[64,4096]{1,0:T(8,128)(2,1)S(1)}, bf16[64,4096]{1,0:T(8,128)(2,1)S(1)}, u32[]{:S(2)}, u32[]{:S(2)}) %collective-permute-start) | collective-permute-done | bytes 524320 | tf_op jit(solution)/shard_map/ppermute | solution.py:10
  69.5 0.2 fusion.13
  69.8 0.0 copy-done.2
  69.8 11.3 %fusion.10 = bf16[1,64,3072]{2,1,0:T(8,128)(2,1)} fusion(bf16[1,4096,3072]{2,1,0:T(8,128)(2,1)} %param.9, bf16[64,4096]{1,0:T(8,128)(2,1)S(1)} %collective-permute-done, f32[4096]{0:T(1024)S(1)} %bitcast.23, f32[64]{0:T(128)S(1)} %add_rsqrt_fusion), kind=kOutput, calls=%fused_computation.6 | convolution fusion | flops 1611857920 | bytes 26099968 | tf_op jit(solution)/shard_map/dot_general | solution.py:36
  (1 shorter events, 0.0 us)
Async XLA Ops:
  7.2 1.2 %copy-start = (bf16[1,64,7168]{2,1,0:T(8,128)(2,1)S(1)}, bf16[1,64,7168]{2,1,0:T(8,128)(2,1)}, u32[]{:S(2)}) copy-start(bf16[1,64,7168]{2,1,0:T(8,128)(2,1)} %param.5) | copy-start | bytes 2752516
  7.2 23.6 %copy-start.1 = (bf16[1,32,4096]{2,1,0:T(8,128)(2,1)S(1)}, bf16[1,32,4096]{2,1,0:T(8,128)(2,1)}, u32[]{:S(2)}) copy-start(bf16[1,32,4096]{2,1,0:T(8,128)(2,1)} %param.6) | copy-start | bytes 786436
  7.2 62.6 %copy-start.2 = (f32[1,4096]{1,0:T(1,128)S(1)}, f32[1,4096]{1,0:T(1,128)}, u32[]{:S(2)}) copy-start(f32[1,4096]{1,0:T(1,128)} %param.7) | copy-start | bytes 49156
  7.2 45.1 %all-reduce.2.cloned.1.call-start = ((), (), s32[]{:S(2)}) async-start(), calls=%async_computation | async-start | bytes 1048576 | tf_op jit(solution)/shard_map/psum | solution.py:27
  53.5 16.0 %collective-permute-start = (bf16[64,4096]{1,0:T(8,128)(2,1)S(1)}, bf16[64,4096]{1,0:T(8,128)(2,1)S(1)}, u32[]{:S(2)}, u32[]{:S(2)}) collective-permute-start(bf16[64,4096]{1,0:T(8,128)(2,1)S(1)} %fusion.16), channel_id=1, source_target_pairs={{0,2},{2,4},{4,6},{6,0},{1,3},{3,5},{5,7},{7,1},{8,10},{10,12},{12... | collective-permute-start | bytes 1572872 | tf_op jit(solution)/shard_map/ppermute | solution.py:10
Sparse Core Ops, SparseCore 0:
  30.9 21.4 all-reduce.1
where the time goes:
time: 88.1 us; the launch traced here: 87.9 us
  matrix products  33.7 us (38%)
  waiting for transfers between devices  32.8 us (37%)
  between operations  14.1 us (16%)
  blocking collectives  2.26 us (3%)
  starting transfers between devices  1.85 us (2%)
  local copies, waits for them, and re-layouts  1.84 us (2%)
  other arithmetic  1.38 us (2%)
    dot_general x1, matrix products, shards(): jnp.dot(hidden_rows, down_local, preferred_element_type=jnp.float32)  22.4 us
    psum x1, waiting for transfers between devices, shards(): lax.psum(jnp.dot(hidden_rows, down_local, preferred_element_type=jnp.floa...  19.3 us
    ppermute x1, waiting for transfers between devices, passed_along(): return lax.ppermute(value, axis, pairs)  13.5 us
    dot_general x1, matrix products, shards(): jnp.dot(normed, qkv_local, preferred_element_type=jnp.float32)  11.3 us
    all_gather x1, blocking collectives, shards(): resid_full = lax.all_gather(resid_rows, 'tensor', axis=0, tiled=True)  2.26 us
    ppermute x1, starting transfers between devices, passed_along(): return lax.ppermute(value, axis, pairs)  1.81 us
  transfers between devices with their start and end apart: 2, of which 2 were waited for; matrix products, arithmetic and copies ran while one was open for 1% of the time, Pallas kernels for 0%

commit v1 on v0

--- a/solution.py
+++ b/solution.py
@@ -1,7 +1,16 @@
+import functools
+
 import jax
 import jax.numpy as jnp
 from jax import lax
+from jax.experimental import pallas as pl
+from jax.experimental.pallas import tpu as pltpu
 from jax.sharding import PartitionSpec as P
+
+EPS = 1e-05
+COLS = 512
+K_BLOCKS = 4
+MESH = pl.DeviceIdType.MESH
 
 
 def passed_along(value, axis, steps):
@@ -12,11 +21,11 @@
 
 def normalize(values, gain_row):
     wide = values.astype(jnp.float32)
-    scaler = lax.rsqrt(jnp.mean(wide * wide, axis=-1, keepdims=True) + 1e-05)
+    scaler = lax.rsqrt(jnp.mean(wide * wide, axis=-1, keepdims=True) + EPS)
     return (wide * scaler * gain_row).astype(jnp.bfloat16)
 
 
-def shards(hidden, residual, norm_gain, down_weight, qkv_weight):
+def plain_shards(hidden, residual, norm_gain, down_weight, qkv_weight):
     hidden_rows = hidden[0]
     resid_rows = residual[0]
     gain_row = norm_gain[0]
@@ -39,7 +48,238 @@
     return (section_output[None], projections[None])
 
 
+def boundary_kernel(
+    pipes,
+    hid_hbm, res_hbm, gain_hbm, down_hbm, qkv_hbm,
+    out_hbm, proj_hbm,
+    hid_v, res_v, gain_v, dbuf, qbuf, group, group_in, stage, x_in, out_v, proj_v, acc_v, sumsq,
+    small_sem, d_sem, q_sem, o_sem, g_send, g_recv, x_send, x_recv,
+):
+    dp = lax.axis_index("dp")
+    pipe = lax.axis_index("pipe")
+    core = lax.axis_index("tensor")
+    other = 1 - core
+    after = lax.rem(pipe + 1, pipes)
+    before = lax.rem(pipe + pipes - 1, pipes)
+
+    tokens, units = hid_v.shape
+    mine, width = res_v.shape
+    chunks = width // COLS
+    depth = units // K_BLOCKS
+    q_cols = qbuf.shape[2]
+    q_parts = q_cols // COLS
+    my_rows = pl.ds(pl.multiple_of(core * mine, mine), mine)
+    other_rows = pl.ds(pl.multiple_of(other * mine, mine), mine)
+
+    def cols(c):
+        return pl.ds(pl.multiple_of(c * COLS, COLS), COLS)
+
+    def down_copy(c, k):
+        return pltpu.make_async_copy(
+            down_hbm.at[0, pl.ds(k * depth, depth), cols(c)], dbuf.at[k], d_sem.at[k]
+        )
+
+    def qkv_copy(j):
+        return pltpu.make_async_copy(
+            qkv_hbm.at[0, pl.ds(pl.multiple_of(j * COLS, COLS), COLS), :], qbuf.at[j], q_sem.at[j]
+        )
+
+    hid_copy = pltpu.make_async_copy(hid_hbm.at[0], hid_v, small_sem.at[0])
+    res_copy = pltpu.make_async_copy(res_hbm.at[0], res_v, small_sem.at[1])
+    gain_copy = pltpu.make_async_copy(gain_hbm, gain_v, small_sem.at[2])
+    hid_copy.start()
+    for k in range(K_BLOCKS):
+        down_copy(0, k).start()
+    res_copy.start()
+    gain_copy.start()
+
+    barrier = pltpu.get_barrier_semaphore()
+    for target in (
+        (dp, pipe, other), (dp, after, core), (dp, after, other), (dp, before, core), (dp, before, other)
+    ):
+        pl.semaphore_signal(barrier, inc=1, device_id=target, device_id_type=MESH)
+
+    def group_copy(c):
+        return pltpu.make_async_remote_copy(
+            src_ref=group.at[c, other_rows],
+            dst_ref=group_in.at[c],
+            send_sem=g_send.at[c],
+            recv_sem=g_recv.at[c],
+            device_id=(dp, pipe, other),
+            device_id_type=MESH,
+        )
+
+    def x_copy(c, to):
+        return pltpu.make_async_remote_copy(
+            src_ref=stage.at[c],
+            dst_ref=x_in.at[c, my_rows],
+            send_sem=x_send.at[to, c],
+            recv_sem=x_recv.at[core, c],
+            device_id=(dp, after, to),
+            device_id_type=MESH,
+        )
+
+    def x_arrival(c, source):
+        rows = pl.ds(source * mine, mine)
+        return pltpu.make_async_remote_copy(
+            src_ref=stage.at[c],
+            dst_ref=x_in.at[c, rows],
+            send_sem=x_send.at[source, c],
+            recv_sem=x_recv.at[source, c],
+            device_id=(dp, after, core),
+            device_id_type=MESH,
+        )
+
+    def finish(c):
+        group_copy(c).wait_recv()
+        total = group[c, my_rows, :].astype(jnp.float32) + group_in[c].astype(jnp.float32)
+        rows = (res_v[:, cols(c)].astype(jnp.float32) + total).astype(jnp.bfloat16)
+        stage[c] = rows
+        out_v[:, cols(c)] = rows
+        for to in range(2):
+            x_copy(c, to).start()
+
+    hid_copy.wait()
+
+    def down_step(c, carry):
+        total = None
+        for k in range(K_BLOCKS):
+            down_copy(c, k).wait()
+            term = jnp.dot(
+                hid_v[:, k * depth:(k + 1) * depth], dbuf[k], preferred_element_type=jnp.float32
+            )
+            total = term if total is None else total + term
+
+            @pl.when(c < chunks - 1)
+            def _():
+                down_copy(c + 1, k).start()
+
+            @pl.when(c == chunks - 1)
+            def _():
+                for j in range(k * chunks // K_BLOCKS, (k + 1) * chunks // K_BLOCKS):
+                    qkv_copy(j).start()
+
+        group[c] = total.astype(jnp.bfloat16)
+
+        @pl.when(c == 0)
+        def _():
+            res_copy.wait()
+            pl.semaphore_wait(barrier, 5)
+
+        group_copy(c).start()
+
+        @pl.when(c >= 1)
+        def _():
+            finish(c - 1)
+
+        return carry
+
+    lax.fori_loop(0, chunks, down_step, 0)
+    gain_copy.wait()
+    acc_v[...] = jnp.zeros_like(acc_v)
+    sumsq[...] = jnp.zeros_like(sumsq)
+
+    def qkv_step(j, carry):
+        for source in range(2):
+            x_arrival(j, source).wait_recv()
+        x = x_in[j].astype(jnp.float32)
+        squares = x * x
+        part = squares[:, :128]
+        for i in range(1, COLS // 128):
+            part = part + squares[:, i * 128:(i + 1) * 128]
+        sumsq[...] += part
+        scaled = (x * gain_v[:, cols(j)]).astype(jnp.bfloat16)
+        qkv_copy(j).wait()
+        for n in range(q_parts):
+            at = slice(n * COLS, (n + 1) * COLS)
+            acc_v[:, at] += jnp.dot(scaled, qbuf[j, :, at], preferred_element_type=jnp.float32)
+
+        @pl.when(j == 0)
+        def _():
+            finish(chunks - 1)
+            pltpu.make_async_copy(out_v, out_hbm.at[0], small_sem.at[0]).start()
+
+        return carry
+
+    lax.fori_loop(0, chunks, qkv_step, 0)
+    scaler = lax.rsqrt(jnp.sum(sumsq[...], axis=-1, keepdims=True) / width + EPS)
+
+    def proj_copy(n):
+        at = pl.ds(n * COLS, COLS)
+        return pltpu.make_async_copy(proj_v.at[:, at], proj_hbm.at[0, :, at], o_sem.at[n])
+
+    for n in range(q_parts):
+        at = slice(n * COLS, (n + 1) * COLS)
+        proj_v[:, at] = (acc_v[:, at] * scaler).astype(jnp.bfloat16)
+        proj_copy(n).start()
+
+    pltpu.make_async_copy(out_v, out_hbm.at[0], small_sem.at[0]).wait()
+
+    def drain(c, carry):
+        group_copy(c).wait_send()
+        for to in range(2):
+            x_copy(c, to).wait_send()
+        return carry
+
+    lax.fori_loop(0, chunks, drain, 0)
+    for n in range(q_parts):
+        proj_copy(n).wait()
+
+
+def kernel_shards(pipes, hidden, residual, norm_gain, down_weight, qkv_weight):
+    tokens, units = hidden.shape[1:]
+    mine, width = residual.shape[1:]
+    q_cols = qkv_weight.shape[2]
+    chunks = width // COLS
+    bf16 = jnp.bfloat16
+    any_space = pl.BlockSpec(memory_space=pl.ANY)
+    flops = 2 * tokens * width * (units + q_cols)
+    return pl.pallas_call(
+        functools.partial(boundary_kernel, pipes),
+        out_shape=(
+            jax.ShapeDtypeStruct((1, mine, width), bf16),
+            jax.ShapeDtypeStruct((1, tokens, q_cols), bf16),
+        ),
+        in_specs=[any_space] * 5,
+        out_specs=(any_space, any_space),
+        scratch_shapes=[
+            pltpu.VMEM((tokens, units), bf16),
+            pltpu.VMEM((mine, width), bf16),
+            pltpu.VMEM((1, width), jnp.float32),
+            pltpu.VMEM((K_BLOCKS, units // K_BLOCKS, COLS), bf16),
+            pltpu.VMEM((chunks, COLS, q_cols), bf16),
+            pltpu.VMEM((chunks, tokens, COLS), bf16),
+            pltpu.VMEM((chunks, mine, COLS), bf16),
+            pltpu.VMEM((chunks, mine, COLS), bf16),
+            pltpu.VMEM((chunks, tokens, COLS), bf16),
+            pltpu.VMEM((mine, width), bf16),
+            pltpu.VMEM((tokens, q_cols), bf16),
+            pltpu.VMEM((tokens, q_cols), jnp.float32),
+            pltpu.VMEM((tokens, 128), jnp.float32),
+            pltpu.SemaphoreType.DMA((3,)),
+            pltpu.SemaphoreType.DMA((K_BLOCKS,)),
+            pltpu.SemaphoreType.DMA((chunks,)),
+            pltpu.SemaphoreType.DMA((q_cols // COLS,)),
+            pltpu.SemaphoreType.DMA((chunks,)),
+            pltpu.SemaphoreType.DMA((chunks,)),
+            pltpu.SemaphoreType.DMA((2, chunks)),
+            pltpu.SemaphoreType.DMA((2, chunks)),
+        ],
+        compiler_params=pltpu.CompilerParams(
+            collective_id=0, has_side_effects=True, vmem_limit_bytes=56 * 1024 * 1024
+        ),
+        cost_estimate=pl.CostEstimate(
+            flops=flops, bytes_accessed=2 * width * (units + q_cols), transcendentals=0
+        ),
+    )(hidden, residual, norm_gain, down_weight, qkv_weight)
+
+
 def solution(mesh):
+    pipes = mesh.shape["pipe"]
+    if mesh.shape["tensor"] == 2 and pipes > 2:
+        shards = functools.partial(kernel_shards, pipes)
+    else:
+        shards = plain_shards
     return jax.shard_map(
         shards,
         mesh=mesh,

time: 88.1 us -> 34 us (0.39)
  matrix products: 33.7 us -> 0 us
  waiting for transfers between devices: 32.8 us -> 0 us
  Pallas kernels: 0 us -> 29.8 us
  between operations: 14.1 us -> 0.64 us
  blocking collectives: 2.26 us -> 0 us
  starting transfers between devices: 1.85 us -> 0 us
  local copies, waits for them, and re-layouts: 1.84 us -> 3.44 us
  other arithmetic: 1.38 us -> 0 us
    dot_general x2 -> x0, matrix products: 33.7 us -> none  [the longest x1 22.4 us: shards(): jnp.dot(hidden_rows, down_local, preferred_element_type=jnp.float32)]
    pallas_call x0 -> x1, Pallas kernels: none -> 29.8 us  [kernel_shards(): pl.pallas_call(functools.partial(boundary_kernel, pipes), out_shape=(jax....]
    psum x1 -> x0, waiting for transfers between devices: 19.3 us -> none  [shards(): lax.psum(jnp.dot(hidden_rows, down_local, preferred_element_type=jnp.floa...]
    ppermute x1 -> x0, waiting for transfers between devices: 13.5 us -> none  [passed_along(): return lax.ppermute(value, axis, pairs)]
    unnamed x6 -> x2, local copies, waits for them, and re-layouts: 1.12 us -> 3.44 us
    all_gather x1 -> x0, blocking collectives: 2.26 us -> none  [shards(): resid_full = lax.all_gather(resid_rows, 'tensor', axis=0, tiled=True)]
    ppermute x1 -> x0, starting transfers between devices: 1.81 us -> none  [passed_along(): return lax.ppermute(value, axis, pairs)]
    convert_element_type x1 -> x0, other arithmetic: 1.16 us -> none  [shards(): full_rows = (resid_full.astype(jnp.float32) + summed).astype(jnp.bfloat16)]
  transfers between devices with their start and end apart: 2 -> 0, of which waited for: 2 -> 0; matrix products, arithmetic and copies ran while one was open for 1% -> 0% of each run, Pallas kernels for 0% -> 0%
where the time goes in v1:
time: 34 us; the launch traced here: 33.8 us
  Pallas kernels  29.8 us (88%)
  local copies, waits for them, and re-layouts  3.44 us (10%)
  between operations  0.64 us (2%)
    pallas_call x1, Pallas kernels, kernel_shards(): pl.pallas_call(functools.partial(boundary_kernel, pipes), out_shape=(jax....  29.8 us
    unnamed x2, local copies, waits for them, and re-layouts  3.44 us

profile of v1, /device:TPU:0, one launch (start us, length us, event | category | flops | bytes accessed | tf_op | source)
XLA Modules:
  0.0 33.8 jit_solution(5261445170063321824)
XLA Ops:
  0.6 29.8 %shard_map.68 = (bf16[1,32,4096]{2,1,0:T(8,128)(2,1)}, bf16[1,64,3072]{2,1,0:T(8,128)(2,1)}) custom-call(bf16[1,64,7168]{2,1,0:T(8,128)(2,1)} %hid_hbm.1, bf16[1,32,4096]{2,1,0:T(8,128)(2,1)} %res_hbm.1, f32[1,4096]{1,0:T(1,128)} %gain_hbm.1, bf16[1,7168,4096]{2,1,0:T(8,128)(2,1)} %down_hbm.1, bf16[1,4096,3072]{2,1,0:T(8,128)(2,1)} %qkv_hbm.1), custom_call_target="tpu_custom_call" | custom-call | flops 5368709120 | bytes 83886080 | tf_op jit(solution)/shard_map/pallas_call | solution.py:237
  30.4 1.7 %copy.9 = bf16[1,32,4096]{2,1,0:T(8,128)(2,1)} copy(bf16[1,32,4096]{2,1,0:T(8,128)(2,1)} %get-tuple-element.4) | data formatting | bytes 524288
  32.1 1.8 %copy.10 = bf16[1,64,3072]{2,1,0:T(8,128)(2,1)} copy(bf16[1,64,3072]{2,1,0:T(8,128)(2,1)} %get-tuple-element.5) | data formatting | bytes 786432

commit v2 on v1

--- a/solution.py
+++ b/solution.py
@@ -10,6 +10,7 @@
 EPS = 1e-05
 COLS = 512
 K_BLOCKS = 4
+RING = 2
 MESH = pl.DeviceIdType.MESH
 
 
@@ -51,9 +52,9 @@
 def boundary_kernel(
     pipes,
     hid_hbm, res_hbm, gain_hbm, down_hbm, qkv_hbm,
-    out_hbm, proj_hbm,
-    hid_v, res_v, gain_v, dbuf, qbuf, group, group_in, stage, x_in, out_v, proj_v, acc_v, sumsq,
-    small_sem, d_sem, q_sem, o_sem, g_send, g_recv, x_send, x_recv,
+    out_v, acc_v, sumsq,
+    hid_v, res_v, gain_v, dbuf, qbuf, group, group_in, stage, x_in,
+    small_sem, h_sem, d_sem, q_sem, g_send, g_recv, x_send, x_recv,
 ):
     dp = lax.axis_index("dp")
     pipe = lax.axis_index("pipe")
@@ -75,23 +76,30 @@
         return pl.ds(pl.multiple_of(c * COLS, COLS), COLS)
 
     def down_copy(c, k):
+        slot = lax.rem(c, RING) * K_BLOCKS + k
         return pltpu.make_async_copy(
-            down_hbm.at[0, pl.ds(k * depth, depth), cols(c)], dbuf.at[k], d_sem.at[k]
-        )
+            down_hbm.at[0, pl.ds(k * depth, depth), cols(c)], dbuf.at[slot], d_sem.at[slot]
+        )
+
+    def hid_copy(k):
+        at = pl.ds(k * depth, depth)
+        return pltpu.make_async_copy(hid_hbm.at[0, :, at], hid_v.at[:, at], h_sem.at[k])
 
     def qkv_copy(j):
         return pltpu.make_async_copy(
             qkv_hbm.at[0, pl.ds(pl.multiple_of(j * COLS, COLS), COLS), :], qbuf.at[j], q_sem.at[j]
         )
 
-    hid_copy = pltpu.make_async_copy(hid_hbm.at[0], hid_v, small_sem.at[0])
-    res_copy = pltpu.make_async_copy(res_hbm.at[0], res_v, small_sem.at[1])
-    gain_copy = pltpu.make_async_copy(gain_hbm, gain_v, small_sem.at[2])
-    hid_copy.start()
+    res_copy = pltpu.make_async_copy(res_hbm.at[0], res_v, small_sem.at[0])
+    gain_copy = pltpu.make_async_copy(gain_hbm, gain_v, small_sem.at[1])
     for k in range(K_BLOCKS):
-        down_copy(0, k).start()
+        hid_copy(k).start()
+        down_copy(jnp.int32(0), k).start()
     res_copy.start()
     gain_copy.start()
+    for c in range(1, RING):
+        for k in range(K_BLOCKS):
+            down_copy(jnp.int32(c), k).start()
 
     barrier = pltpu.get_barrier_semaphore()
     for target in (
@@ -139,25 +147,29 @@
         for to in range(2):
             x_copy(c, to).start()
 
-    hid_copy.wait()
-
     def down_step(c, carry):
         total = None
         for k in range(K_BLOCKS):
+
+            @pl.when(c == 0)
+            def _():
+                hid_copy(k).wait()
+
             down_copy(c, k).wait()
             term = jnp.dot(
-                hid_v[:, k * depth:(k + 1) * depth], dbuf[k], preferred_element_type=jnp.float32
+                hid_v[:, k * depth:(k + 1) * depth],
+                dbuf[lax.rem(c, RING) * K_BLOCKS + k],
+                preferred_element_type=jnp.float32,
             )
             total = term if total is None else total + term
 
-            @pl.when(c < chunks - 1)
+            @pl.when(c < chunks - RING)
             def _():
-                down_copy(c + 1, k).start()
-
-            @pl.when(c == chunks - 1)
+                down_copy(c + RING, k).start()
+
+            @pl.when(c >= chunks - RING)
             def _():
-                for j in range(k * chunks // K_BLOCKS, (k + 1) * chunks // K_BLOCKS):
-                    qkv_copy(j).start()
+                qkv_copy((c - (chunks - RING)) * K_BLOCKS + k).start()
 
         group[c] = total.astype(jnp.bfloat16)
 
@@ -197,23 +209,10 @@
         @pl.when(j == 0)
         def _():
             finish(chunks - 1)
-            pltpu.make_async_copy(out_v, out_hbm.at[0], small_sem.at[0]).start()
 
         return carry
 
     lax.fori_loop(0, chunks, qkv_step, 0)
-    scaler = lax.rsqrt(jnp.sum(sumsq[...], axis=-1, keepdims=True) / width + EPS)
-
-    def proj_copy(n):
-        at = pl.ds(n * COLS, COLS)
-        return pltpu.make_async_copy(proj_v.at[:, at], proj_hbm.at[0, :, at], o_sem.at[n])
-
-    for n in range(q_parts):
-        at = slice(n * COLS, (n + 1) * COLS)
-        proj_v[:, at] = (acc_v[:, at] * scaler).astype(jnp.bfloat16)
-        proj_copy(n).start()
-
-    pltpu.make_async_copy(out_v, out_hbm.at[0], small_sem.at[0]).wait()
 
     def drain(c, carry):
         group_copy(c).wait_send()
@@ -222,8 +221,23 @@
         return carry
 
     lax.fori_loop(0, chunks, drain, 0)
-    for n in range(q_parts):
-        proj_copy(n).wait()
+
+
+def write_kernel(rows_v, acc_v, sumsq, out_hbm, proj_hbm, proj_v, r_sem, o_sem):
+    width = rows_v.shape[1]
+    q_cols = acc_v.shape[1]
+    rows_copy = pltpu.make_async_copy(rows_v, out_hbm.at[0], r_sem)
+    rows_copy.start()
+    scaler = lax.rsqrt(jnp.sum(sumsq[...], axis=-1, keepdims=True) / width + EPS)
+    copies = []
+    for n in range(q_cols // COLS):
+        at = slice(n * COLS, (n + 1) * COLS)
+        proj_v[:, at] = (acc_v[:, at] * scaler).astype(jnp.bfloat16)
+        copy = pltpu.make_async_copy(proj_v.at[:, at], proj_hbm.at[0, :, at], o_sem.at[n])
+        copy.start()
+        copies.append(copy)
+    for copy in [rows_copy] + copies:
+        copy.wait()
 
 
 def kernel_shards(pipes, hidden, residual, norm_gain, down_weight, qkv_weight):
@@ -234,32 +248,30 @@
     bf16 = jnp.bfloat16
     any_space = pl.BlockSpec(memory_space=pl.ANY)
     flops = 2 * tokens * width * (units + q_cols)
-    return pl.pallas_call(
+    vmem_space = pl.BlockSpec(memory_space=pltpu.VMEM)
+    rows, acc, sumsq = pl.pallas_call(
         functools.partial(boundary_kernel, pipes),
         out_shape=(
-            jax.ShapeDtypeStruct((1, mine, width), bf16),
-            jax.ShapeDtypeStruct((1, tokens, q_cols), bf16),
+            pltpu.VMEM((mine, width), bf16),
+            pltpu.VMEM((tokens, q_cols), jnp.float32),
+            pltpu.VMEM((tokens, 128), jnp.float32),
         ),
         in_specs=[any_space] * 5,
-        out_specs=(any_space, any_space),
+        out_specs=(vmem_space,) * 3,
         scratch_shapes=[
             pltpu.VMEM((tokens, units), bf16),
             pltpu.VMEM((mine, width), bf16),
             pltpu.VMEM((1, width), jnp.float32),
-            pltpu.VMEM((K_BLOCKS, units // K_BLOCKS, COLS), bf16),
+            pltpu.VMEM((RING * K_BLOCKS, units // K_BLOCKS, COLS), bf16),
             pltpu.VMEM((chunks, COLS, q_cols), bf16),
             pltpu.VMEM((chunks, tokens, COLS), bf16),
             pltpu.VMEM((chunks, mine, COLS), bf16),
             pltpu.VMEM((chunks, mine, COLS), bf16),
             pltpu.VMEM((chunks, tokens, COLS), bf16),
-            pltpu.VMEM((mine, width), bf16),
-            pltpu.VMEM((tokens, q_cols), bf16),
-            pltpu.VMEM((tokens, q_cols), jnp.float32),
-            pltpu.VMEM((tokens, 128), jnp.float32),
-            pltpu.SemaphoreType.DMA((3,)),
+            pltpu.SemaphoreType.DMA((2,)),
             pltpu.SemaphoreType.DMA((K_BLOCKS,)),
+            pltpu.SemaphoreType.DMA((RING * K_BLOCKS,)),
             pltpu.SemaphoreType.DMA((chunks,)),
-            pltpu.SemaphoreType.DMA((q_cols // COLS,)),
             pltpu.SemaphoreType.DMA((chunks,)),
             pltpu.SemaphoreType.DMA((chunks,)),
             pltpu.SemaphoreType.DMA((2, chunks)),
@@ -272,6 +284,20 @@
             flops=flops, bytes_accessed=2 * width * (units + q_cols), transcendentals=0
         ),
     )(hidden, residual, norm_gain, down_weight, qkv_weight)
+    return pl.pallas_call(
+        write_kernel,
+        out_shape=(
+            jax.ShapeDtypeStruct((1, mine, width), bf16),
+            jax.ShapeDtypeStruct((1, tokens, q_cols), bf16),
+        ),
+        in_specs=[vmem_space] * 3,
+        out_specs=(any_space, any_space),
+        scratch_shapes=[
+            pltpu.VMEM((tokens, q_cols), bf16),
+            pltpu.SemaphoreType.DMA,
+            pltpu.SemaphoreType.DMA((q_cols // COLS,)),
+        ],
+    )(rows, acc, sumsq)
 
 
 def solution(mesh):

time: 34 us -> 34 us (level)
  local copies, waits for them, and re-layouts: 3.44 us -> 2.18 us
  Pallas kernels: 29.8 us -> 31 us
    pallas_call x1 -> x2, Pallas kernels: 29.8 us -> 31 us  [the longest x1 29 us: kernel_shards(): pl.pallas_call(functools.partial(boundary_kernel, pipes), out_shape=(pltp...]
    unnamed x2 -> x6, local copies, waits for them, and re-layouts: 3.44 us -> 2.18 us
where the time goes in v2:
time: 34 us; the launch traced here: 33.9 us
  Pallas kernels  31 us (91%)
  local copies, waits for them, and re-layouts  2.18 us (6%)
  between operations  0.65 us (2%)
    pallas_call x1, Pallas kernels, kernel_shards(): pl.pallas_call(functools.partial(boundary_kernel, pipes), out_shape=(pltp...  29 us
    unnamed x6, local copies, waits for them, and re-layouts  2.18 us
    pallas_call x1, Pallas kernels, kernel_shards(): pl.pallas_call(write_kernel, out_shape=(jax.ShapeDtypeStruct((1, mine, wi...  2.08 us

profile of v2, /device:TPU:0, one launch (start us, length us, event | category | flops | bytes accessed | tf_op | source)
XLA Modules:
  0.0 33.9 jit_solution(9681842175555845764)
XLA Ops:
  0.6 29.0 %shard_map.68 = (bf16[32,4096]{1,0:T(8,128)(2,1)S(1)}, f32[64,3072]{1,0:T(8,128)S(1)}, f32[64,128]{1,0:T(8,128)S(1)}) custom-call(bf16[1,64,7168]{2,1,0:T(8,128)(2,1)} %hid_hbm.1, bf16[1,32,4096]{2,1,0:T(8,128)(2,1)} %res_hbm.1, f32[1,4096]{1,0:T(1,128)} %gain_hbm.1, bf16[1,7168,4096]{2,1,0:T(8,128)(2,1)} %down_hbm.1, bf16[1,4096,3072]{2,1,0:T(8,128)(2,1)} %qkv_hbm.1), custom_call_target="tpu_custom_call" | custom-call | flops 5368709120 | bytes 83886080 | tf_op jit(solution)/shard_map/pallas_call | solution.py:252
  29.6 0.0 copy-start
  29.6 0.9 %copy-done = f32[64,3072]{1,0:T(8,128)} copy-done((f32[64,3072]{1,0:T(8,128)}, f32[64,3072]{1,0:T(8,128)S(1)}, u32[]{:S(2)}) %copy-start) | copy-done | bytes 786456
  30.5 0.0 copy-start.1
  30.5 0.7 %copy-done.1 = bf16[32,4096]{1,0:T(8,128)(2,1)} copy-done((bf16[32,4096]{1,0:T(8,128)(2,1)}, bf16[32,4096]{1,0:T(8,128)(2,1)S(1)}, u32[]{:S(2)}) %copy-start.1) | copy-done | bytes 262168
  31.2 0.0 copy-start.2
  31.2 0.6 %copy-done.2 = f32[64,128]{1,0:T(8,128)} copy-done((f32[64,128]{1,0:T(8,128)}, f32[64,128]{1,0:T(8,128)S(1)}, u32[]{:S(2)}) %copy-start.2) | copy-done | bytes 32792
  31.8 2.1 %shard_map.69 = (bf16[1,32,4096]{2,1,0:T(8,128)(2,1)}, bf16[1,64,3072]{2,1,0:T(8,128)(2,1)}) custom-call(bf16[32,4096]{1,0:T(8,128)(2,1)} %copy-done.1, f32[64,3072]{1,0:T(8,128)} %copy-done, f32[64,128]{1,0:T(8,128)} %copy-done.2), custom_call_target="tpu_custom_call" | custom-call | tf_op jit(solution)/shard_map/pallas_call | solution.py:287
Async XLA Ops:
  29.6 0.9 %copy-start = (f32[64,3072]{1,0:T(8,128)}, f32[64,3072]{1,0:T(8,128)S(1)}, u32[]{:S(2)}) copy-start(f32[64,3072]{1,0:T(8,128)S(1)} %get-tuple-element.6.acc_v) | copy-start | bytes 2359300
  30.5 0.7 %copy-start.1 = (bf16[32,4096]{1,0:T(8,128)(2,1)}, bf16[32,4096]{1,0:T(8,128)(2,1)S(1)}, u32[]{:S(2)}) copy-start(bf16[32,4096]{1,0:T(8,128)(2,1)S(1)} %get-tuple-element.5.rows_v) | copy-start | bytes 786436
  31.2 0.6 %copy-start.2 = (f32[64,128]{1,0:T(8,128)}, f32[64,128]{1,0:T(8,128)S(1)}, u32[]{:S(2)}) copy-start(f32[64,128]{1,0:T(8,128)S(1)} %get-tuple-element.7.sumsq) | copy-start | bytes 98308

commit v3 on v2

--- a/solution.py
+++ b/solution.py
@@ -69,6 +69,7 @@
     depth = units // K_BLOCKS
     q_cols = qbuf.shape[2]
     q_parts = q_cols // COLS
+    q_half = q_cols // 2
     my_rows = pl.ds(pl.multiple_of(core * mine, mine), mine)
     other_rows = pl.ds(pl.multiple_of(other * mine, mine), mine)
 
@@ -85,9 +86,10 @@
         at = pl.ds(k * depth, depth)
         return pltpu.make_async_copy(hid_hbm.at[0, :, at], hid_v.at[:, at], h_sem.at[k])
 
-    def qkv_copy(j):
+    def qkv_copy(j, half):
+        at = pl.ds(half * q_half, q_half)
         return pltpu.make_async_copy(
-            qkv_hbm.at[0, pl.ds(pl.multiple_of(j * COLS, COLS), COLS), :], qbuf.at[j], q_sem.at[j]
+            qkv_hbm.at[0, cols(j), at], qbuf.at[j, :, at], q_sem.at[half, j]
         )
 
     res_copy = pltpu.make_async_copy(res_hbm.at[0], res_v, small_sem.at[0])
@@ -169,7 +171,8 @@
 
             @pl.when(c >= chunks - RING)
             def _():
-                qkv_copy((c - (chunks - RING)) * K_BLOCKS + k).start()
+                for half in range(2):
+                    qkv_copy((c - (chunks - RING)) * K_BLOCKS + k, half).start()
 
         group[c] = total.astype(jnp.bfloat16)
 
@@ -201,8 +204,9 @@
             part = part + squares[:, i * 128:(i + 1) * 128]
         sumsq[...] += part
         scaled = (x * gain_v[:, cols(j)]).astype(jnp.bfloat16)
-        qkv_copy(j).wait()
         for n in range(q_parts):
+            if n * COLS % q_half == 0:
+                qkv_copy(j, n * COLS // q_half).wait()
             at = slice(n * COLS, (n + 1) * COLS)
             acc_v[:, at] += jnp.dot(scaled, qbuf[j, :, at], preferred_element_type=jnp.float32)
 
@@ -271,7 +275,7 @@
             pltpu.SemaphoreType.DMA((2,)),
             pltpu.SemaphoreType.DMA((K_BLOCKS,)),
             pltpu.SemaphoreType.DMA((RING * K_BLOCKS,)),
-            pltpu.SemaphoreType.DMA((chunks,)),
+            pltpu.SemaphoreType.DMA((2, chunks)),
             pltpu.SemaphoreType.DMA((chunks,)),
             pltpu.SemaphoreType.DMA((chunks,)),
             pltpu.SemaphoreType.DMA((2, chunks)),
@@ -297,7 +301,8 @@
             pltpu.SemaphoreType.DMA,
             pltpu.SemaphoreType.DMA((q_cols // COLS,)),
         ],
-    )(rows, acc, sumsq)
+        compiler_params=pltpu.CompilerParams(vmem_limit_bytes=8 * 1024 * 1024),
+    )(*(pltpu.with_memory_space_constraint(held, pltpu.VMEM) for held in (rows, acc, sumsq)))
 
 
 def solution(mesh):

time: 34 us -> 30.7 us (0.903)
  local copies, waits for them, and re-layouts: 2.18 us -> 0 us
  Pallas kernels: 31 us -> 30 us
    unnamed x6 -> x0, local copies, waits for them, and re-layouts: 2.18 us -> none
    pallas_call x1, Pallas kernels: 2.08 us -> 0.89 us  [kernel_shards(): pl.pallas_call(write_kernel, out_shape=(jax.ShapeDtypeStruct((1, mine, wi...]
where the time goes in v3:
time: 30.7 us; the launch traced here: 30.6 us
  Pallas kernels  30 us (98%)
  between operations  0.64 us (2%)
    pallas_call x1, Pallas kernels, kernel_shards(): pl.pallas_call(functools.partial(boundary_kernel, pipes), out_shape=(pltp...  29.1 us
    pallas_call x1, Pallas kernels, kernel_shards(): pl.pallas_call(write_kernel, out_shape=(jax.ShapeDtypeStruct((1, mine, wi...  0.89 us

profile of v3, /device:TPU:0, one launch (start us, length us, event | category | flops | bytes accessed | tf_op | source)
XLA Modules:
  0.0 30.6 jit_solution(8041333752635100134)
XLA Ops:
  0.6 29.1 %shard_map.68 = (bf16[32,4096]{1,0:T(8,128)(2,1)S(1)}, f32[64,3072]{1,0:T(8,128)S(1)}, f32[64,128]{1,0:T(8,128)S(1)}) custom-call(bf16[1,64,7168]{2,1,0:T(8,128)(2,1)} %hid_hbm.1, bf16[1,32,4096]{2,1,0:T(8,128)(2,1)} %res_hbm.1, f32[1,4096]{1,0:T(1,128)} %gain_hbm.1, bf16[1,7168,4096]{2,1,0:T(8,128)(2,1)} %down_hbm.1, bf16[1,4096,3072]{2,1,0:T(8,128)(2,1)} %qkv_hbm.1), custom_call_target="tpu_custom_call" | custom-call | flops 5368709120 | bytes 83886080 | tf_op jit(solution)/shard_map/pallas_call | solution.py:256
  29.7 0.9 %shard_map.69 = (bf16[1,32,4096]{2,1,0:T(8,128)(2,1)}, bf16[1,64,3072]{2,1,0:T(8,128)(2,1)}) custom-call(bf16[32,4096]{1,0:T(8,128)(2,1)S(1)} %get-tuple-element.5.rows_v, f32[64,3072]{1,0:T(8,128)S(1)} %get-tuple-element.6.acc_v, f32[64,128]{1,0:T(8,128)S(1)} %get-tuple-element.7.sumsq), custom_call_target="tpu_custom_call" | custom-call | tf_op jit(solution)/shard_map/pallas_call | solution.py:291

commit v4 on v3

--- a/solution.py
+++ b/solution.py
@@ -190,6 +190,7 @@
         return carry
 
     lax.fori_loop(0, chunks, down_step, 0)
+    finish(chunks - 1)
     gain_copy.wait()
     acc_v[...] = jnp.zeros_like(acc_v)
     sumsq[...] = jnp.zeros_like(sumsq)
@@ -209,10 +210,6 @@
                 qkv_copy(j, n * COLS // q_half).wait()
             at = slice(n * COLS, (n + 1) * COLS)
             acc_v[:, at] += jnp.dot(scaled, qbuf[j, :, at], preferred_element_type=jnp.float32)
-
-        @pl.when(j == 0)
-        def _():
-            finish(chunks - 1)
 
         return carry
 

time: 30.7 us -> 30.7 us (level)
  no operation moved by 1% of the time
where the time goes in v4:
time: 30.7 us; the launch traced here: 30.6 us
  Pallas kernels  30 us (98%)
  between operations  0.64 us (2%)
    pallas_call x1, Pallas kernels, kernel_shards(): pl.pallas_call(functools.partial(boundary_kernel, pipes), out_shape=(pltp...  29.1 us
    pallas_call x1, Pallas kernels, kernel_shards(): pl.pallas_call(write_kernel, out_shape=(jax.ShapeDtypeStruct((1, mine, wi...  0.89 us

profile of v4, /device:TPU:0, one launch (start us, length us, event | category | flops | bytes accessed | tf_op | source)
XLA Modules:
  0.0 30.6 jit_solution(9581105588817471814)
XLA Ops:
  0.6 29.1 %shard_map.68 = (bf16[32,4096]{1,0:T(8,128)(2,1)S(1)}, f32[64,3072]{1,0:T(8,128)S(1)}, f32[64,128]{1,0:T(8,128)S(1)}) custom-call(bf16[1,64,7168]{2,1,0:T(8,128)(2,1)} %hid_hbm.1, bf16[1,32,4096]{2,1,0:T(8,128)(2,1)} %res_hbm.1, f32[1,4096]{1,0:T(1,128)} %gain_hbm.1, bf16[1,7168,4096]{2,1,0:T(8,128)(2,1)} %down_hbm.1, bf16[1,4096,3072]{2,1,0:T(8,128)(2,1)} %qkv_hbm.1), custom_call_target="tpu_custom_call" | custom-call | flops 5368709120 | bytes 83886080 | tf_op jit(solution)/shard_map/pallas_call | solution.py:253
  29.7 0.9 %shard_map.69 = (bf16[1,32,4096]{2,1,0:T(8,128)(2,1)}, bf16[1,64,3072]{2,1,0:T(8,128)(2,1)}) custom-call(bf16[32,4096]{1,0:T(8,128)(2,1)S(1)} %get-tuple-element.5.rows_v, f32[64,3072]{1,0:T(8,128)S(1)} %get-tuple-element.6.acc_v, f32[64,128]{1,0:T(8,128)S(1)} %get-tuple-element.7.sumsq), custom_call_target="tpu_custom_call" | custom-call | tf_op jit(solution)/shard_map/pallas_call | solution.py:288
